TPU v7x, 32 devices: a whole 2x2x4 slice. The times are simulated.
32 devices in a mesh: dp: 4 (over z), block: 8 (over y, x, core).
Axes of the slice: x: 2, y: 2, z: 4, core: 2. Of those that a mesh axis runs over, the one named last changes fastest.
Arguments:
- tokens: bfloat16 [4096, 5120], P('dp', 'block'), may hold values from -6 to 6
- up_left: bfloat16 [128, 40, 160], P('block'), may hold values from -1 to 1
- up_right: bfloat16 [160, 128, 128], P('block'), may hold values from -0.5 to 0.5
- down_left: bfloat16 [160, 128, 128], P('block'), may hold values from -0.5 to 0.5
- down_right: bfloat16 [128, 160, 40], P('block'), may hold values from -0.5 to 0.5
- cotangent: bfloat16 [4096, 5120], P('dp', 'block'), may hold values from -6 to 6
Outputs:
- output: bfloat16 [4096, 5120], P('dp', 'block')
- grad_tokens: bfloat16 [4096, 5120], P('dp', 'block')
- grad_up_left: float32 [128, 40, 160], P('block')
- grad_up_right: float32 [160, 128, 128], P('block')
- grad_down_left: float32 [160, 128, 128], P('block')
- grad_down_right: float32 [128, 160, 40], P('block')
All inputs are finite; a program needn't handle non-finite values.
Results may differ from a plain program's by a relative error of at most 0.007.
Values may be sent and summed in bfloat16 or wider, within the bound.
A program may use at most 192 MiB of HBM per device.

v0:
```python
import jax
import jax.numpy as jnp
from jax import lax
from jax.sharding import PartitionSpec as P

root_half = 0.7071067811865476
gauss_norm = 0.3989422804014327


def gelu_exact(value):
    return 0.5 * value * (1.0 + lax.erf(value * root_half))


def gelu_slope(value):
    return (
        0.5 * (1.0 + lax.erf(value * root_half))
        + value * jnp.exp(-0.5 * value * value) * gauss_norm
    )


def forward(tokens_in, up_left, up_right, down_left, down_right):
    rows = tokens_in.shape[0]
    split_in = tokens_in.reshape(rows, up_left.shape[0], up_left.shape[1])
    first = jnp.einsum(
        "tia,iaj->ijt", split_in, up_left, preferred_element_type=jnp.float32
    ).astype(jnp.bfloat16)
    piece = lax.all_to_all(first, "block", split_axis=1, concat_axis=0, tiled=True)
    mixed_in = piece
    pre_act = jnp.einsum("ijt,jim->jmt", piece, up_right, preferred_element_type=jnp.float32)
    hidden = gelu_exact(pre_act).astype(jnp.bfloat16)
    second = jnp.einsum(
        "jkt,jkl->ljt", hidden, down_left, preferred_element_type=jnp.float32
    ).astype(jnp.bfloat16)
    piece = lax.all_to_all(second, "block", split_axis=0, concat_axis=1, tiled=True)
    result = jnp.einsum(
        "ljt,ljo->lot", piece, down_right, preferred_element_type=jnp.float32
    ).astype(jnp.bfloat16)
    return (result, split_in, mixed_in, pre_act, hidden, piece)


def on_device(tokens, up_left, up_right, down_left, down_right, cotangent):
    rows = tokens.shape[0]
    result, split_in, mixed_in, pre_act, hidden, mixed_out = forward(
        tokens, up_left, up_right, down_left, down_right
    )
    output = jnp.transpose(result, (2, 0, 1)).reshape(rows, -1)
    again, _ = lax.optimization_barrier((tokens, output))
    _, split_in, mixed_in, pre_act, hidden, mixed_out = forward(
        again, up_left, up_right, down_left, down_right
    )
    grad_out = cotangent.reshape(rows, down_right.shape[0], down_right.shape[2])
    grad_dr = jnp.einsum("ljt,tlo->ljo", mixed_out, grad_out, preferred_element_type=jnp.float32)
    grad_second = jnp.einsum(
        "tlo,ljo->ljt", grad_out, down_right, preferred_element_type=jnp.float32
    ).astype(jnp.bfloat16)
    grad_back = lax.all_to_all(grad_second, "block", split_axis=1, concat_axis=0, tiled=True)
    grad_dl = jnp.einsum("jkt,ljt->jkl", hidden, grad_back, preferred_element_type=jnp.float32)
    grad_hidden = jnp.einsum(
        "ljt,jkl->jkt", grad_back, down_left, preferred_element_type=jnp.float32
    )
    grad_pre = (grad_hidden * gelu_slope(pre_act)).astype(jnp.bfloat16)
    grad_ur = jnp.einsum("ijt,jmt->jim", mixed_in, grad_pre, preferred_element_type=jnp.float32)
    grad_first = jnp.einsum(
        "jmt,jim->ijt", grad_pre, up_right, preferred_element_type=jnp.float32
    ).astype(jnp.bfloat16)
    grad_front = lax.all_to_all(grad_first, "block", split_axis=0, concat_axis=1, tiled=True)
    grad_ul = jnp.einsum("tia,ijt->iaj", split_in, grad_front, preferred_element_type=jnp.float32)
    grad_x = jnp.einsum(
        "ijt,iaj->tia", grad_front, up_left, preferred_element_type=jnp.float32
    ).astype(jnp.bfloat16)
    grad_ul, grad_ur, grad_dl, grad_dr = lax.psum((grad_ul, grad_ur, grad_dl, grad_dr), "dp")
    return (output, grad_x.reshape(rows, -1), grad_ul, grad_ur, grad_dl, grad_dr)


def solution(mesh):
    return jax.shard_map(
        on_device,
        mesh=mesh,
        in_specs=(
            P("dp", "block"),
            P("block", None, None),
            P("block", None, None),
            P("block", None, None),
            P("block", None, None),
            P("dp", "block"),
        ),
        out_specs=(
            P("dp", "block"),
            P("dp", "block"),
            P("block", None, None),
            P("block", None, None),
            P("block", None, None),
            P("block", None, None),
        ),
        check_vma=False,
    )
```

profile of v0, /device:TPU:2, one launch (start us, length us, event | category | flops | bytes accessed | tf_op | source)
XLA Modules:
  0.0 648.8 jit_solution(11823484331618309042)
XLA Ops:
  7.2 0.0 copy-start
  7.2 1.7 copy.55
  8.9 2.5 convolution_convert_fusion.1
  11.4 2.9 copy.56
  14.3 62.9 %all_to_all.108 = bf16[16,160,1024]{2,0,1:T(8,128)(2,1)S(1)} all-to-all(bf16[16,160,1024]{2,0,1:T(8,128)(2,1)S(1)} %copy.56), channel_id=1, replica_groups=mesh['dp'=4,'block'=8] {'block'}, dimensions={1} | all-to-all | bytes 10485760 | tf_op jit(solution)/shard_map/all_to_all | solution.py:27
  77.2 3.0 copy.57
  80.2 0.0 copy-done
  80.2 0.0 copy-done.11
  80.2 7.5 %convert_bitcast_fusion.3 = bf16[128,20,1024]{0,2,1:T(8,128)(2,1)} fusion(bf16[20,128,128]{2,1,0:T(8,128)(2,1)S(1)} %copy-done.11, bf16[128,20,1024]{2,0,1:T(8,128)(2,1)} %bitcast.93, bf16[20,128,128]{2,1,0:T(8,128)(2,1)S(1)} %copy-done), kind=kOutput, calls=%fused_computation.21 | convolution fusion | flops 1357905920 | bytes 11796480 | tf_op jit(solution)/shard_map/jkt,jkl->ljt/dot_general | solution.py:31
  87.7 8.6 %copy.59 = bf16[128,20,1024]{2,1,0:T(8,128)(2,1)} copy(bf16[128,20,1024]{0,2,1:T(8,128)(2,1)} %convert_bitcast_fusion.3) | data formatting | bytes 10485760 | tf_op jit(solution)/shard_map/convert_element_type | solution.py:33
  96.3 75.4 %all_to_all.109 = bf16[128,20,1024]{2,1,0:T(8,128)(2,1)S(1)} all-to-all(bf16[128,20,1024]{2,1,0:T(8,128)(2,1)} %copy.59), channel_id=1, replica_groups=mesh['dp'=4,'block'=8] {'block'}, dimensions={0} | all-to-all | bytes 10485760 | tf_op jit(solution)/shard_map/all_to_all | solution.py:34
  171.7 3.1 copy.61
  174.9 0.0 copy-start.7
  174.9 0.0 copy-done.14
  174.9 6.8 %fusion.22 = bf16[16,1024,40]{1,2,0:T(8,128)(2,1)} fusion(bf16[16,160,40]{1,2,0:T(8,128)(2,1)S(1)} %copy-done.14, bf16[16,160,1024]{2,0,1:T(8,128)(2,1)S(1)} %bitcast.94), kind=kOutput, calls=%fused_computation.30 | convolution fusion | flops 210370560 | bytes 6758400 | tf_op jit(solution)/shard_map/ljt,ljo->lot/dot_general | solution.py:35
  181.7 0.0 copy-done.7
  181.7 1.1 copy.67
  182.7 2.5 convert_bitcast_fusion.2
  185.3 5.3 copy.68
  190.5 6.0 all-to-all-start.3
  196.6 1.6 copy.63
  198.2 2.5 convolution_convert_fusion
  200.7 5.2 copy.64
  205.9 49.6 %all-to-all-done.3 = bf16[16,160,1024]{2,0,1:T(8,128)(2,1)} async-done(((bf16[16,160,1024]{2,0,1:T(8,128)(2,1)}), bf16[16,160,1024]{2,0,1:T(8,128)(2,1)}, u32[]{:S(2)}, u32[]{:S(2)}) %all-to-all-start.3) | async-done | bytes 5242912 | tf_op jit(solution)/shard_map/all_to_all | solution.py:27
  255.5 6.1 all-to-all-start.2
  261.6 3.1 copy.69
  264.7 0.0 copy-start.1
  264.7 0.0 copy-start.12
  264.7 6.3 fusion.9
  271.0 0.0 copy-done.1
  271.0 2.4 copy-done.2
  273.3 0.0 copy-done.12
  273.3 3.2 convert_bitcast_fusion
  276.5 8.6 %copy.78 = bf16[128,20,1024]{2,1,0:T(8,128)(2,1)} copy(bf16[128,20,1024]{0,2,1:T(8,128)(2,1)} %convert_bitcast_fusion) | data formatting | bytes 10485760 | tf_op jit(solution)/shard_map/convert_element_type | solution.py:33
  285.1 35.5 %all-to-all-done.2 = bf16[16,160,1024]{2,0,1:T(8,128)(2,1)} async-done(((bf16[16,160,1024]{2,0,1:T(8,128)(2,1)}), bf16[16,160,1024]{2,0,1:T(8,128)(2,1)}, u32[]{:S(2)}, u32[]{:S(2)}) %all-to-all-start.2) | async-done | bytes 5242912 | tf_op jit(solution)/shard_map/all_to_all | solution.py:56
  320.5 6.2 all-to-all-start.5
  326.7 3.2 copy.65
  329.9 9.9 %fusion.5 = bf16[20,128,1024]{1,2,0:T(8,128)(2,1)S(1)} fusion(f32[20,1024,128]{2,1,0:T(8,128)} %get-tuple-element.31, bf16[128,20,1024]{2,0,1:T(8,128)(2,1)S(1)} %bitcast.87, bf16[20,128,128]{2,1,0:T(8,128)(2,1)S(1)} %copy-done.13), kind=kOutput, calls=%fused_computation.6 | convolution fusion | flops 697303040 | bytes 21626880 | tf_op jit(solution)/shard_map/ljt,jkl->jkt/dot_general | solution.py:58
  339.9 2.3 copy-done.3
  342.2 3.2 convert_bitcast_fusion.1
  345.4 8.5 %copy.71 = bf16[128,20,1024]{2,1,0:T(8,128)(2,1)} copy(bf16[128,20,1024]{0,2,1:T(8,128)(2,1)} %convert_bitcast_fusion.1) | data formatting | bytes 10485760 | tf_op jit(solution)/shard_map/convert_element_type | solution.py:65
  353.9 43.0 %all-to-all-done.5 = bf16[128,20,1024]{2,1,0:T(8,128)(2,1)} async-done(((bf16[128,20,1024]{2,1,0:T(8,128)(2,1)}), bf16[128,20,1024]{2,1,0:T(8,128)(2,1)}, u32[]{:S(2)}, u32[]{:S(2)}) %all-to-all-start.5) | async-done | bytes 5242912 | tf_op jit(solution)/shard_map/all_to_all | solution.py:34
  396.9 6.1 all-to-all-start.4
  403.1 0.2 all-reduce.3.cloned.1.call-start
  403.2 6.9 %fusion.31 = f32[20,128,128]{2,1,0:T(8,128)} fusion(bf16[20,128,1024]{1,2,0:T(8,128)(2,1)} %copy-done.2, bf16[128,20,1024]{2,0,1:T(8,128)(2,1)} %bitcast.88), kind=kOutput, calls=%fused_computation.36 | convolution fusion | flops 671088640 | bytes 11796480 | tf_op jit(solution)/shard_map/jkt,ljt->jkl/dot_general | solution.py:57
  410.1 0.0 copy-done.4
  410.1 5.2 fusion.30
  415.3 5.9 copy.80
  421.2 4.0 fusion.10
  425.2 48.0 %all-to-all-done.4 = bf16[128,20,1024]{2,1,0:T(8,128)(2,1)} async-done(((bf16[128,20,1024]{2,1,0:T(8,128)(2,1)}), bf16[128,20,1024]{2,1,0:T(8,128)(2,1)}, u32[]{:S(2)}, u32[]{:S(2)}) %all-to-all-start.4) | async-done | bytes 5242912 | tf_op jit(solution)/shard_map/all_to_all | solution.py:66
  473.3 6.1 copy.73
  479.4 2.3 copy-done.6
  481.7 4.1 fusion.15
  485.8 0.0 all-reduce.3.cloned.1.call-update
  485.8 1.4 copy.82
  487.2 0.0 copy-done.9
  487.2 8.2 %fusion.19 = bf16[16,1024,40]{1,2,0:T(8,128)(2,1)S(1)} fusion(bf16[16,40,160]{2,1,0:T(8,128)(2,1)S(1)} %copy-done.9, bf16[16,160,1024]{2,0,1:T(8,128)(2,1)} %bitcast.91), kind=kOutput, calls=%fused_computation.29 | convolution fusion | flops 210370560 | bytes 6758400 | tf_op jit(solution)/shard_map/ijt,iaj->tia/dot_general | solution.py:68
  495.5 1.4 copy.83
  496.9 137.0 %all-reduce.3.cloned.1.call-done = (f32[16,40,160]{2,1,0:T(8,128)}, f32[20,128,128]{2,1,0:T(8,128)}, f32[20,128,128]{2,1,0:T(8,128)}, f32[16,160,40]{1,2,0:T(8,128)}) async-done(((f32[16,40,160]{2,1,0:T(8,128)}, f32[20,128,128]{2,1,0:T(8,128)}, f32[20,128,128]{2,1,0:T(8,128)}, f32[16,160,40]{1,2,0:T(8,128)}), (f32[16,40,160]{2,1,0:T(8,128)}, f32[20,128,128]{2,1,0:T(8,128)}, f32[20,128,128]{2,1,0:T(8,128)}, ...) | async-done | bytes 3440656 | tf_op jit(solution)/shard_map/psum | solution.py:71
  633.9 2.0 copy.108
  635.9 2.5 copy.109
  638.4 2.5 copy.110
  640.9 0.0 copy-done.10
  640.9 0.8 copy.111
  (14 shorter events, 0.0 us)
Async XLA Ops:
  7.2 73.0 %copy-start = (bf16[20,128,128]{2,1,0:T(8,128)(2,1)S(1)}, bf16[20,128,128]{2,1,0:T(8,128)(2,1)}, u32[]{:S(2)}) copy-start(bf16[20,128,128]{2,1,0:T(8,128)(2,1)} %param.8) | copy-start | bytes 1966084
  77.2 3.0 copy-start.11
  171.7 3.1 copy-start.14
  174.9 6.8 %copy-start.7 = (bf16[1024,640]{1,0:T(8,128)(2,1)S(1)}, bf16[1024,640]{1,0:T(8,128)(2,1)}, u32[]{:S(2)}) copy-start(bf16[1024,640]{1,0:T(8,128)(2,1)} %param.6) | copy-start | bytes 3932164
  190.5 65.0 %all-to-all-start.3 = ((bf16[16,160,1024]{2,0,1:T(8,128)(2,1)}), bf16[16,160,1024]{2,0,1:T(8,128)(2,1)}, u32[]{:S(2)}, u32[]{:S(2)}) async-start(bf16[16,160,1024]{2,0,1:T(8,128)(2,1)} %copy.68), calls=%async_computation.3 | async-start | bytes 10485760 | tf_op jit(solution)/shard_map/all_to_all | solution.py:27
  255.5 65.0 %all-to-all-start.2 = ((bf16[16,160,1024]{2,0,1:T(8,128)(2,1)}), bf16[16,160,1024]{2,0,1:T(8,128)(2,1)}, u32[]{:S(2)}, u32[]{:S(2)}) async-start(bf16[16,160,1024]{2,0,1:T(8,128)(2,1)} %copy.64), calls=%async_computation.2 | async-start | bytes 10485760 | tf_op jit(solution)/shard_map/all_to_all | solution.py:56
  264.7 6.3 copy-start.1
  264.7 8.7 %copy-start.12 = (bf16[20,128,128]{2,1,0:T(8,128)(2,1)S(1)}, bf16[20,128,128]{2,1,0:T(8,128)(2,1)}, u32[]{:S(2)}) copy-start(bf16[20,128,128]{2,1,0:T(8,128)(2,1)} %param.9) | copy-start | bytes 1966084
  271.0 2.4 copy-start.2
  320.5 76.4 %all-to-all-start.5 = ((bf16[128,20,1024]{2,1,0:T(8,128)(2,1)}), bf16[128,20,1024]{2,1,0:T(8,128)(2,1)}, u32[]{:S(2)}, u32[]{:S(2)}) async-start(bf16[128,20,1024]{2,1,0:T(8,128)(2,1)} %copy.78), calls=%async_computation.5 | async-start | bytes 12582912 | tf_op jit(solution)/shard_map/all_to_all | solution.py:34
  326.7 3.2 copy-start.13
  329.9 9.9 %copy-start.5 = (bf16[8,16,20,1024]{3,1,0,2:T(8,128)(2,1)}, bf16[8,16,20,1024]{3,1,0,2:T(8,128)(2,1)S(1)}, u32[]{:S(2)}) copy-start(bf16[8,16,20,1024]{3,1,0,2:T(8,128)(2,1)S(1)} %copy.65) | copy-start | bytes 15728644
  339.9 2.3 copy-start.3
  396.9 76.3 %all-to-all-start.4 = ((bf16[128,20,1024]{2,1,0:T(8,128)(2,1)}), bf16[128,20,1024]{2,1,0:T(8,128)(2,1)}, u32[]{:S(2)}, u32[]{:S(2)}) async-start(bf16[128,20,1024]{2,1,0:T(8,128)(2,1)} %copy.71), calls=%async_computation.4 | async-start | bytes 12582912 | tf_op jit(solution)/shard_map/all_to_all | solution.py:66
  403.1 230.8 %all-reduce.3.cloned.1.call-start = ((), (), s32[]{:S(2)}) async-start(), calls=%async_computation.6 | async-start | bytes 7864320 | tf_op jit(solution)/shard_map/psum | solution.py:71
  403.2 6.9 %copy-start.4 = (bf16[20,128,1024]{1,2,0:T(8,128)(2,1)S(1)}, bf16[20,128,1024]{1,2,0:T(8,128)(2,1)}, u32[]{:S(2)}) copy-start(bf16[20,128,1024]{1,2,0:T(8,128)(2,1)} %copy-done.3) | copy-start | bytes 15728644
  479.4 2.3 copy-start.6
  481.7 4.1 copy-start.8
  485.8 1.5 copy-start.9
  633.9 7.0 %copy-start.10 = (f32[16,160,40]{1,2,0:T(8,128)S(1)}, f32[16,160,40]{1,2,0:T(8,128)}, u32[]{:S(2)}) copy-start(f32[16,160,40]{1,2,0:T(8,128)} %get-tuple-element.37) | copy-start | bytes 1228804
Sparse Core Ops, SparseCore 0:
  485.9 147.9 all-reduce.2
where the time goes:
time: 657 us; the launch traced here: 649 us
  waiting for transfers between devices  313 us (48%)
  blocking collectives  138 us (21%)
  local copies, waits for them, and re-layouts  85.7 us (13%)
  matrix products  72.8 us (11%)
  starting transfers between devices  24.6 us (4%)
  between operations  14.5 us (2%)
    psum x1, waiting for transfers between devices, on_device(): lax.psum((grad_ul, grad_ur, grad_dl, grad_dr), 'dp')  137 us
    all_to_all x1, blocking collectives, forward(): lax.all_to_all(second, 'block', split_axis=0, concat_axis=1, tiled=True)  75.4 us
    all_to_all x1, blocking collectives, forward(): lax.all_to_all(first, 'block', split_axis=1, concat_axis=0, tiled=True)  62.9 us
    all_to_all x1, waiting for transfers between devices, forward(): lax.all_to_all(first, 'block', split_axis=1, concat_axis=0, tiled=True)  49.6 us
    all_to_all x1, waiting for transfers between devices, on_device(): lax.all_to_all(grad_first, 'block', split_axis=0, concat_axis=1, tiled=True)  48 us
    all_to_all x1, waiting for transfers between devices, forward(): lax.all_to_all(second, 'block', split_axis=0, concat_axis=1, tiled=True)  43 us
    all_to_all x1, waiting for transfers between devices, on_device(): lax.all_to_all(grad_second, 'block', split_axis=1, concat_axis=0, tiled=T...  35.5 us
    unnamed x38, local copies, waits for them, and re-layouts  21.1 us
  transfers between devices with their start and end apart: 5, of which 5 were waited for; matrix products, arithmetic and copies ran while one was open for 14% of the time, Pallas kernels for 0%

commit v1 on v0

v1 whole, which is shorter than its diff:
```python
import jax
import jax.numpy as jnp
from jax import lax
from jax.sharding import PartitionSpec as P

root_half = 0.7071067811865476
gauss_norm = 0.3989422804014327
F32, BF16 = jnp.float32, jnp.bfloat16


def gelu_exact(value):
    return 0.5 * value * (1.0 + lax.erf(value * root_half))


def gelu_slope(value):
    return (
        0.5 * (1.0 + lax.erf(value * root_half))
        + value * jnp.exp(-0.5 * value * value) * gauss_norm
    )


def mul(spec, a, b):
    return jnp.einsum(spec, a, b, preferred_element_type=F32)


def swap(piece, n, bit):
    return lax.ppermute(piece, "block", [(d, d ^ bit) for d in range(n)])


def orders(n):
    bits = [1 << p for p in range(1, n.bit_length() - 1)]
    return bits, bits[::-1]


def gather(halves, n):
    have = [{0: half} for half in halves]
    for step in range(len(orders(n)[0])):
        for h, order in enumerate(orders(n)):
            for k in sorted(have[h]):
                have[h][k ^ order[step]] = swap(have[h][k], n, order[step])
    for h in range(2):
        for k in list(have[h]):
            have[h][k ^ 1] = swap(have[h][k], n, 1)
    return have


def scatter(parts, n):
    def fold(pieces, bit):
        return {
            k: (pieces[k].astype(F32) + swap(pieces[k ^ bit], n, bit).astype(F32)).astype(BF16)
            for k in sorted(pieces)
            if not k & bit
        }

    now = [fold(pieces, 1) for pieces in parts]
    for step in range(len(orders(n)[0])):
        now = [fold(now[h], order[step]) for h, order in enumerate(orders(n))]
    return jnp.concatenate([now[0][0], now[1][0]], axis=0)


def make_on_device(n):
    def on_device(tokens, up_left, up_right, down_left, down_right, cotangent):
        me = lax.axis_index("block")
        rows = tokens.shape[0]
        bi, aw, mb = up_left.shape
        own, bs, half = mb // n, up_right.shape[1], bi // 2
        xt = tokens.T.reshape(bi, aw, rows)
        ct = cotangent.T.reshape(bi, aw, rows)

        outer = jnp.stack([jnp.transpose(up_left, (0, 2, 1)), down_right])
        outer = jnp.transpose(outer.reshape(2 * bi, n, own * aw), (1, 0, 2))
        outer = lax.all_to_all(outer, "block", split_axis=0, concat_axis=0, tiled=True)
        outer = [
            lax.dynamic_index_in_dim(outer, me ^ k, 0, keepdims=False).reshape(2, bi, own, aw)
            for k in range(n)
        ]
        index = jnp.arange(bs)
        target = ((index // bi) ^ me) * bi + index % bi
        perm = (index[:, None] == target[None, :]).astype(BF16)
        ur = mul("jim,ip->jpm", up_right, perm).astype(BF16)
        dl = mul("jkl,lp->jkp", down_left, perm).astype(BF16)

        x = gather((xt[:half], xt[half:]), n)
        ct, *_ = lax.optimization_barrier(
            (ct, x[0][orders(n)[0][0]], x[1][orders(n)[1][0]])
        )
        c = gather((ct[:half], ct[half:]), n)

        def outer_of(which, h, k):
            return outer[k][which, h * half : (h + 1) * half]

        def cut(array, h, k):
            return array[k * bi + h * half : k * bi + (h + 1) * half]

        def every(make):
            return jnp.concatenate([make(h, k) for k in range(n) for h in range(2)], axis=0)

        first = every(lambda h, k: mul("iat,ija->ijt", x[h][k], outer_of(0, h, k)).astype(BF16))
        pre_act = mul("ijt,jim->jmt", first, ur)
        hidden = gelu_exact(pre_act).astype(BF16)
        second = mul("jkt,jkl->ljt", hidden, dl).astype(BF16)
        out = [
            {
                k: mul("ljt,ljo->lot", cut(second, h, k), outer_of(1, h, k)).astype(BF16)
                for k in range(n)
            }
            for h in range(2)
        ]
        output = scatter(out, n).reshape(bi * aw, rows).T

        grad_second = every(
            lambda h, k: mul("lot,ljo->ljt", c[h][k], outer_of(1, h, k)).astype(BF16)
        )
        grad_hidden = mul("ljt,jkl->jkt", grad_second, dl)
        grad_pre = (grad_hidden * gelu_slope(pre_act)).astype(BF16)
        grad_first = mul("jmt,jim->ijt", grad_pre, ur).astype(BF16)
        gx = [
            {
                k: mul("ijt,ija->iat", cut(grad_first, h, k), outer_of(0, h, k)).astype(BF16)
                for k in range(n)
            }
            for h in range(2)
        ]
        grad_x = scatter(gx, n).reshape(bi * aw, rows).T

        grad_dl = mul("jkt,ljt->jkl", hidden, grad_second).astype(BF16)
        grad_ur = mul("ijt,jmt->jim", first, grad_pre).astype(BF16)
        grad_dl = mul("jkp,lp->jkl", grad_dl, perm).astype(BF16)
        grad_ur = mul("jpm,ip->jim", grad_ur, perm).astype(BF16)
        grad_dl, grad_ur = lax.psum((grad_dl, grad_ur), "dp")
        grad_dr = every(lambda h, k: mul("ljt,lot->ljo", cut(second, h, k), c[h][k]).astype(BF16))
        grad_ul = every(
            lambda h, k: mul("ijt,iat->ija", cut(grad_first, h, k), x[h][k]).astype(BF16)
        )
        both = jnp.concatenate(
            [grad_ul.reshape(n, bi, own * aw), grad_dr.reshape(n, bi, own * aw)], axis=1
        )
        both = jnp.concatenate(
            [lax.dynamic_index_in_dim(both, me ^ k, 0, keepdims=True) for k in range(n)], axis=0
        )
        both = lax.all_to_all(both, "block", split_axis=0, concat_axis=0, tiled=True)
        both = lax.psum(both, "dp").astype(F32).reshape(n, 2, bi, own, aw)
        grad_ul = jnp.transpose(both[:, 0], (1, 3, 0, 2)).reshape(bi, aw, mb)
        grad_dr = jnp.transpose(both[:, 1], (1, 0, 2, 3)).reshape(bi, mb, aw)
        return (output, grad_x, grad_ul, grad_ur.astype(F32), grad_dl.astype(F32), grad_dr)

    return on_device


def solution(mesh):
    return jax.shard_map(
        make_on_device(mesh.shape["block"]),
        mesh=mesh,
        in_specs=(
            P("dp", "block"),
            P("block", None, None),
            P("block", None, None),
            P("block", None, None),
            P("block", None, None),
            P("dp", "block"),
        ),
        out_specs=(
            P("dp", "block"),
            P("dp", "block"),
            P("block", None, None),
            P("block", None, None),
            P("block", None, None),
            P("block", None, None),
        ),
        check_vma=False,
    )
```

time: 657 us -> 415 us (0.63)
  waiting for transfers between devices: 313 us -> 123 us
  blocking collectives: 138 us -> 0 us
  matrix products: 72.8 us -> 174 us
  local copies, waits for them, and re-layouts: 85.7 us -> 43.1 us
  other arithmetic: 0 us -> 16.8 us
  starting transfers between devices: 24.6 us -> 36.2 us
    all_to_all x4 -> x2, waiting for transfers between devices: 176 us -> 21.1 us  [the longest x1 21.1 us: on_device(): lax.all_to_all(outer, 'block', split_axis=0, concat_axis=0, tiled=True)]
    all_to_all x2 -> x0, blocking collectives: 138 us -> none  [the longest x1 75.4 us: forward(): lax.all_to_all(second, 'block', split_axis=0, concat_axis=1, tiled=True)]
    psum x1, waiting for transfers between devices: 137 us -> 19.8 us  [on_device(): both = lax.psum(both, 'dp').astype(F32).reshape(n, 2, bi, own, aw)]
    dot_general x14 -> x104, matrix products: 72.8 us -> 174 us  [mul(): return jnp.einsum(spec, a, b, preferred_element_type=F32)]
    ppermute x0 -> x56, waiting for transfers between devices: none -> 82.3 us  [swap(): return lax.ppermute(piece, 'block', [(d, d ^ bit) for d in range(n)])]
    convert_element_type x6 -> x0, local copies, waits for them, and re-layouts: 39.1 us -> none  [the longest x2 17.2 us: forward(): second = jnp.einsum('jkt,jkl->ljt', hidden, down_left, preferred_element_...]
    ppermute x0 -> x56, starting transfers between devices: none -> 27.1 us  [swap(): return lax.ppermute(piece, 'block', [(d, d ^ bit) for d in range(n)])]
    all_to_all x6 -> x0, local copies, waits for them, and re-layouts: 24.4 us -> none  [the longest x2 9.01 us: forward(): lax.all_to_all(second, 'block', split_axis=0, concat_axis=1, tiled=True)]
  transfers between devices with their start and end apart: 5 -> 59, of which waited for: 5 -> 13; matrix products, arithmetic and copies ran while one was open for 14% -> 54% of each run, Pallas kernels for 0% -> 0%
where the time goes in v1:
time: 415 us; the launch traced here: 409 us
  matrix products  174 us (42%)
  waiting for transfers between devices  123 us (30%)
  local copies, waits for them, and re-layouts  43.1 us (10%)
  starting transfers between devices  36.2 us (9%)
  other arithmetic  16.8 us (4%)
  between operations  15.5 us (4%)
    dot_general x104, matrix products, mul(): return jnp.einsum(spec, a, b, preferred_element_type=F32)  174 us
    ppermute x56, waiting for transfers between devices, swap(): return lax.ppermute(piece, 'block', [(d, d ^ bit) for d in range(n)])  82.3 us
    ppermute x56, starting transfers between devices, swap(): return lax.ppermute(piece, 'block', [(d, d ^ bit) for d in range(n)])  27.1 us
    all_to_all x1, waiting for transfers between devices, on_device(): lax.all_to_all(outer, 'block', split_axis=0, concat_axis=0, tiled=True)  21.1 us
    psum x1, waiting for transfers between devices, on_device(): both = lax.psum(both, 'dp').astype(F32).reshape(n, 2, bi, own, aw)  19.8 us
    unnamed x190, local copies, waits for them, and re-layouts  12.2 us
    convert_element_type x8, other arithmetic, fold(): (pieces[k].astype(F32) + swap(pieces[k ^ bit], n, bit).astype(F32)).astyp...  11.4 us
    reshape x8, local copies, waits for them, and re-layouts, on_device(): lax.dynamic_index_in_dim(outer, me ^ k, 0, keepdims=False)  9.57 us
  transfers between devices with their start and end apart: 59, of which 13 were waited for; matrix products, arithmetic and copies ran while one was open for 54% of the time, Pallas kernels for 0%

profile of v1, /device:TPU:2, one launch (start us, length us, event | category | flops | bytes accessed | tf_op | source)
XLA Modules:
  0.0 408.6 jit_solution(544320426662555788)
XLA Ops:
  7.2 1.8 fusion.219
  12.6 1.9 collective-permute-start.3
  18.0 4.5 %all-to-all-start = ((bf16[8,32,800]{2,1,0:T(8,128)(2,1)}), bf16[8,32,800]{2,1,0:T(8,128)(2,1)}, u32[]{:S(2)}, u32[]{:S(2)}) async-start(bf16[8,32,800]{2,1,0:T(8,128)(2,1)} %copy.286), calls=%async_computation | async-start | bytes 917504 | tf_op jit(solution)/shard_map/all_to_all | solution.py:72
  23.4 1.6 copy.310
  25.0 21.1 %all-to-all-done = bf16[8,32,800]{2,1,0:T(8,128)(2,1)} async-done(((bf16[8,32,800]{2,1,0:T(8,128)(2,1)}), bf16[8,32,800]{2,1,0:T(8,128)(2,1)}, u32[]{:S(2)}, u32[]{:S(2)}) %all-to-all-start) | async-done | bytes 409632 | tf_op jit(solution)/shard_map/all_to_all | solution.py:72
  46.1 1.7 constant_dynamic-slice_fusion
  51.5 1.7 reshape.104
  53.2 1.7 reshape.103
  54.9 1.7 reshape.102
  57.4 1.8 fusion.86
  59.2 2.1 fusion.85
  64.4 2.1 fusion.84
  68.2 2.1 fusion.82
  70.3 2.1 fusion.81
  76.8 2.1 fusion.78
  78.9 2.1 fusion.77
  85.2 8.4 %collective-permute-done.30 = bf16[8,40,1024]{2,1,0:T(8,128)(2,1)} collective-permute-done((bf16[8,40,1024]{2,1,0:T(8,128)(2,1)S(1)}, bf16[8,40,1024]{2,1,0:T(8,128)(2,1)}, u32[]{:S(2)}, u32[]{:S(2)}) %collective-permute-start.30) | collective-permute-done | bytes 655392 | tf_op jit(solution)/shard_map/ppermute | solution.py:27
  93.6 2.1 fusion.66
  95.7 2.1 fusion.65
  99.7 4.3 %collective-permute-done.10 = bf16[8,40,1024]{2,1,0:T(8,128)(2,1)S(1)} collective-permute-done((bf16[8,40,1024]{2,1,0:T(8,128)(2,1)}, bf16[8,40,1024]{2,1,0:T(8,128)(2,1)S(1)}, u32[]{:S(2)}, u32[]{:S(2)}) %collective-permute-start.10) | collective-permute-done | bytes 655392 | tf_op jit(solution)/shard_map/ppermute | solution.py:27
  104.1 3.1 collective-permute-done.11
  114.4 6.3 %multiply_convert_fusion = (bf16[20,128,1024]{2,1,0:T(8,128)(2,1)S(1)}, f32[20,128,1024]{2,1,0:T(8,128)S(1)}) fusion(bf16[20,128,128]{2,1,0:T(8,128)(2,1)S(1)} %fusion.53, bf16[128,20,1024]{2,1,0:T(8,128)(2,1)} %fusion.71), kind=kOutput, calls=%fused_computation.7 | convolution fusion | flops 684195840 | bytes 21626880 | tf_op jit(solution)/shard_map/ijt,jim->jmt/dot_general | solution.py:23
  137.9 2.1 fusion.63
  140.0 2.1 fusion.62
  142.1 2.1 fusion.61
  149.3 2.7 collective-permute-done.38
  152.1 2.1 fusion.59
  155.2 2.1 fusion.57
  174.2 7.7 %fusion.5 = bf16[20,128,1024]{2,1,0:T(8,128)(2,1)S(1)} fusion(f32[20,128,1024]{2,1,0:T(8,128)S(1)} %get-tuple-element.76, bf16[20,128,128]{1,2,0:T(8,128)(2,1)S(1)} %fusion.54, bf16[128,20,1024]{2,1,0:T(8,128)(2,1)} %fusion.55), kind=kOutput, calls=%fused_computation.6 | convolution fusion | flops 697303040 | bytes 21626880 | tf_op jit(solution)/shard_map/ljt,jkl->jkt/dot_general | solution.py:23
  187.9 2.1 fusion.117
  198.2 2.1 fusion.116
  201.3 2.2 fusion.114
  203.5 2.1 fusion.113
  207.7 2.2 fusion.110
  209.9 2.2 fusion.109
  218.2 1.7 reshape.112
  220.0 2.2 fusion.88
  223.2 1.7 reshape.113
  233.3 4.5 %all-to-all-start.1 = ((bf16[8,32,800]{2,1,0:T(8,128)(2,1)}), bf16[8,32,800]{2,1,0:T(8,128)(2,1)S(1)}, u32[]{:S(2)}, u32[]{:S(2)}) async-start(bf16[8,32,800]{2,1,0:T(8,128)(2,1)} %constant_dynamic-update-slice_fusion.2), calls=%async_computation.1 | async-start | bytes 917504 | tf_op jit(solution)/shard_map/all_to_all | solution.py:141
  237.9 2.4 fusion.41
  240.4 2.4 add_convert_fusion.19
  243.2 2.4 add_convert_fusion.16
  245.6 9.1 %fusion.31 = bf16[20,128,128]{2,1,0:T(8,128)(2,1)} fusion(bf16[20,128,1024]{2,1,0:T(8,128)(2,1)} %copy-done.2, bf16[128,20,1024]{2,1,0:T(8,128)(2,1)} %fusion.55, s32[128]{0:T(128)S(1)} %fusion.209), kind=kOutput, calls=%fused_computation.26 | convolution fusion | flops 755646464 | bytes 11141632 | tf_op jit(solution)/shard_map/jkp,lp->jkl/dot_general | solution.py:23
  256.2 2.4 add_convert_fusion.26
  258.6 8.9 %fusion.50 = bf16[20,128,128]{2,1,0:T(8,128)(2,1)} fusion(bf16[20,128,1024]{2,1,0:T(8,128)(2,1)} %copy-done.3, bf16[128,20,1024]{2,1,0:T(8,128)(2,1)} %fusion.71, s32[128]{0:T(128)S(1)} %fusion.209), kind=kOutput, calls=%fused_computation.107 | convolution fusion | flops 755646464 | bytes 11141632 | tf_op jit(solution)/shard_map/jpm,ip->jim/dot_general | solution.py:23
  267.6 2.5 add_convert_fusion.23
  270.0 2.1 convolution_convert_fusion.11
  272.2 2.1 convolution_convert_fusion.3
  277.3 2.6 reshape.114
  280.9 2.4 add_convert_fusion.12
  283.3 1.7 add_convert_fusion.15
  285.7 1.7 add_convert_fusion.2
  288.0 9.5 %collective-permute-done.19 = bf16[8,40,1024]{2,1,0:T(8,128)(2,1)S(1)} collective-permute-done((bf16[8,40,1024]{2,1,0:T(8,128)(2,1)}, bf16[8,40,1024]{2,1,0:T(8,128)(2,1)S(1)}, u32[]{:S(2)}, u32[]{:S(2)}) %collective-permute-start.19) | collective-permute-done | bytes 655392 | tf_op jit(solution)/shard_map/ppermute | solution.py:27
  300.4 2.3 collective-permute-done.23
  306.2 9.9 %collective-permute-done.54 = bf16[8,40,1024]{2,1,0:T(8,128)(2,1)S(1)} collective-permute-done((bf16[8,40,1024]{2,1,0:T(8,128)(2,1)S(1)}, bf16[8,40,1024]{2,1,0:T(8,128)(2,1)S(1)}, u32[]{:S(2)}, u32[]{:S(2)}) %collective-permute-start.54) | collective-permute-done | bytes 655392 | tf_op jit(solution)/shard_map/ppermute | solution.py:27
  321.0 8.7 %collective-permute-done.47 = bf16[8,40,1024]{2,1,0:T(8,128)(2,1)S(1)} collective-permute-done((bf16[8,40,1024]{2,1,0:T(8,128)(2,1)S(1)}, bf16[8,40,1024]{2,1,0:T(8,128)(2,1)S(1)}, u32[]{:S(2)}, u32[]{:S(2)}) %collective-permute-start.47) | collective-permute-done | bytes 655392 | tf_op jit(solution)/shard_map/ppermute | solution.py:27
  331.2 12.6 %collective-permute-done.16 = bf16[8,40,1024]{2,1,0:T(8,128)(2,1)S(1)} collective-permute-done((bf16[8,40,1024]{2,1,0:T(8,128)(2,1)S(1)}, bf16[8,40,1024]{2,1,0:T(8,128)(2,1)S(1)}, u32[]{:S(2)}, u32[]{:S(2)}) %collective-permute-start.16) | collective-permute-done | bytes 655392 | tf_op jit(solution)/shard_map/ppermute | solution.py:27
  344.1 1.7 collective-permute-start.48
  347.9 10.0 %collective-permute-done.55 = bf16[8,40,1024]{2,1,0:T(8,128)(2,1)} collective-permute-done((bf16[8,40,1024]{2,1,0:T(8,128)(2,1)}, bf16[8,40,1024]{2,1,0:T(8,128)(2,1)}, u32[]{:S(2)}, u32[]{:S(2)}) %collective-permute-start.55) | collective-permute-done | bytes 655392 | tf_op jit(solution)/shard_map/ppermute | solution.py:27
  357.9 1.9 add_convert_fusion
  359.8 10.6 %collective-permute-done.44 = bf16[8,40,1024]{2,1,0:T(8,128)(2,1)} collective-permute-done((bf16[8,40,1024]{2,1,0:T(8,128)(2,1)}, bf16[8,40,1024]{2,1,0:T(8,128)(2,1)}, u32[]{:S(2)}, u32[]{:S(2)}) %collective-permute-start.44) | collective-permute-done | bytes 655392 | tf_op jit(solution)/shard_map/ppermute | solution.py:27
  370.4 2.0 add_convert_fusion.7
  373.9 19.8 %all-reduce.3.cloned.1.call-done = (bf16[8,2,16,20,40]{4,3,2,1,0:T(8,128)(2,1)}, bf16[20,128,128]{2,1,0:T(8,128)(2,1)}, bf16[20,128,128]{2,1,0:T(8,128)(2,1)}) async-done(((bf16[8,2,16,20,40]{4,3,2,1,0:T(8,128)(2,1)}, bf16[20,128,128]{2,1,0:T(8,128)(2,1)}, bf16[20,128,128]{2,1,0:T(8,128)(2,1)}), (bf16[8,2,16,20,40]{4,3,2,1,0:T(8,128)(2,1)}, bf16[20,128,128]{2,1,0:T(8,128)(2,1)}, ...) | async-done | bytes 1720336 | tf_op jit(solution)/shard_map/psum | solution.py:142
  393.7 2.4 convert_element_type.786
  (393 shorter events, 136.4 us)
Async XLA Ops:
  9.3 66.7 %collective-permute-start.6 = (bf16[8,40,1024]{2,1,0:T(8,128)(2,1)S(1)}, bf16[8,40,1024]{2,1,0:T(8,128)(2,1)}, u32[]{:S(2)}, u32[]{:S(2)}) collective-permute-start(bf16[8,40,1024]{2,1,0:T(8,128)(2,1)S(1)} %bitcast.253), channel_id=1, source_target_pairs={{0,4},{1,5},{2,6},{3,7},{4,0},{5,1},{6,2},{7,3},{8,12},{9,13},{10,... | collective-permute-start | bytes 1966088 | tf_op jit(solution)/shard_map/ppermute | solution.py:27
  10.9 50.5 %collective-permute-start.2 = (bf16[8,40,1024]{2,1,0:T(8,128)(2,1)S(1)}, bf16[8,40,1024]{2,1,0:T(8,128)(2,1)}, u32[]{:S(2)}, u32[]{:S(2)}) collective-permute-start(bf16[8,40,1024]{2,1,0:T(8,128)(2,1)S(1)} %bitcast.254), channel_id=1, source_target_pairs={{0,2},{1,3},{2,0},{3,1},{4,6},{5,7},{6,4},{7,5},{8,10},{9,11},{10,... | collective-permute-start | bytes 1966088 | tf_op jit(solution)/shard_map/ppermute | solution.py:27
  11.4 53.0 %collective-permute-start = (bf16[8,40,1024]{2,1,0:T(8,128)(2,1)S(1)}, bf16[8,40,1024]{2,1,0:T(8,128)(2,1)}, u32[]{:S(2)}, u32[]{:S(2)}) collective-permute-start(bf16[8,40,1024]{2,1,0:T(8,128)(2,1)S(1)} %bitcast.255), channel_id=1, source_target_pairs={{0,1},{1,0},{2,3},{3,2},{4,5},{5,4},{6,7},{7,6},{8,9},{9,8},{10,11... | collective-permute-start | bytes 1966088 | tf_op jit(solution)/shard_map/ppermute | solution.py:27
  12.5 48.9 %collective-permute-start.7 = (bf16[8,40,1024]{2,1,0:T(8,128)(2,1)}, bf16[8,40,1024]{2,1,0:T(8,128)(2,1)}, u32[]{:S(2)}, u32[]{:S(2)}) collective-permute-start(bf16[8,40,1024]{2,1,0:T(8,128)(2,1)} %bitcast.13), channel_id=1, source_target_pairs={{0,4},{1,5},{2,6},{3,7},{4,0},{5,1},{6,2},{7,3},{8,12},{9,13},{10,... | collective-permute-start | bytes 1966088 | tf_op jit(solution)/shard_map/ppermute | solution.py:27
  12.6 53.9 %collective-permute-start.3 = (bf16[8,40,1024]{2,1,0:T(8,128)(2,1)}, bf16[8,40,1024]{2,1,0:T(8,128)(2,1)}, u32[]{:S(2)}, u32[]{:S(2)}) collective-permute-start(bf16[8,40,1024]{2,1,0:T(8,128)(2,1)} %bitcast.13), channel_id=1, source_target_pairs={{0,2},{1,3},{2,0},{3,1},{4,6},{5,7},{6,4},{7,5},{8,10},{9,11},{10,... | collective-permute-start | bytes 1966088 | tf_op jit(solution)/shard_map/ppermute | solution.py:27
  18.0 28.1 %all-to-all-start = ((bf16[8,32,800]{2,1,0:T(8,128)(2,1)}), bf16[8,32,800]{2,1,0:T(8,128)(2,1)}, u32[]{:S(2)}, u32[]{:S(2)}) async-start(bf16[8,32,800]{2,1,0:T(8,128)(2,1)} %copy.286), calls=%async_computation | async-start | bytes 917504 | tf_op jit(solution)/shard_map/all_to_all | solution.py:72
  61.4 5.7 %collective-permute-start.1 = (bf16[8,40,1024]{2,1,0:T(8,128)(2,1)}, bf16[8,40,1024]{2,1,0:T(8,128)(2,1)S(1)}, u32[]{:S(2)}, u32[]{:S(2)}) collective-permute-start(bf16[8,40,1024]{2,1,0:T(8,128)(2,1)} %bitcast.13), channel_id=1, source_target_pairs={{0,1},{1,0},{2,3},{3,2},{4,5},{5,4},{6,7},{7,6},{8,9},{9,8},{10,11... | collective-permute-start | bytes 1966088 | tf_op jit(solution)/shard_map/ppermute | solution.py:27
  61.5 23.0 %collective-permute-start.31 = (bf16[8,40,1024]{2,1,0:T(8,128)(2,1)S(1)}, bf16[8,40,1024]{2,1,0:T(8,128)(2,1)}, u32[]{:S(2)}, u32[]{:S(2)}) collective-permute-start(bf16[8,40,1024]{2,1,0:T(8,128)(2,1)S(1)} %get-tuple-element.63), channel_id=1, source_target_pairs={{0,2},{1,3},{2,0},{3,1},{4,6},{5,7},{6,4},{7,5},{8,10},{9,11},{10,... | collective-permute-start | bytes 1966088 | tf_op jit(solution)/shard_map/ppermute | solution.py:27
  64.4 17.9 %collective-permute-start.29 = (bf16[8,40,1024]{2,1,0:T(8,128)(2,1)S(1)}, bf16[8,40,1024]{2,1,0:T(8,128)(2,1)S(1)}, u32[]{:S(2)}, u32[]{:S(2)}) collective-permute-start(bf16[8,40,1024]{2,1,0:T(8,128)(2,1)S(1)} %get-tuple-element.63), channel_id=1, source_target_pairs={{0,1},{1,0},{2,3},{3,2},{4,5},{5,4},{6,7},{7,6},{8,9},{9,8},{10,11... | collective-permute-start | bytes 1966088 | tf_op jit(solution)/shard_map/ppermute | solution.py:27
  66.5 5.9 %collective-permute-start.4 = (bf16[8,40,1024]{2,1,0:T(8,128)(2,1)}, bf16[8,40,1024]{2,1,0:T(8,128)(2,1)S(1)}, u32[]{:S(2)}, u32[]{:S(2)}) collective-permute-start(bf16[8,40,1024]{2,1,0:T(8,128)(2,1)} %collective-permute-done.2), channel_id=1, source_target_pairs={{0,1},{1,0},{2,3},{3,2},{4,5},{5,4},{6,7},{7,6},{8,9},{9,8},{10,11... | collective-permute-start | bytes 1966088 | tf_op jit(solution)/shard_map/ppermute | solution.py:27
  67.1 7.9 %collective-permute-start.5 = (bf16[8,40,1024]{2,1,0:T(8,128)(2,1)}, bf16[8,40,1024]{2,1,0:T(8,128)(2,1)S(1)}, u32[]{:S(2)}, u32[]{:S(2)}) collective-permute-start(bf16[8,40,1024]{2,1,0:T(8,128)(2,1)} %collective-permute-done.3), channel_id=1, source_target_pairs={{0,1},{1,0},{2,3},{3,2},{4,5},{5,4},{6,7},{7,6},{8,9},{9,8},{10,11... | collective-permute-start | bytes 1966088 | tf_op jit(solution)/shard_map/ppermute | solution.py:27
  72.4 35.3 %collective-permute-start.35 = (bf16[8,40,1024]{2,1,0:T(8,128)(2,1)S(1)}, bf16[8,40,1024]{2,1,0:T(8,128)(2,1)}, u32[]{:S(2)}, u32[]{:S(2)}) collective-permute-start(bf16[8,40,1024]{2,1,0:T(8,128)(2,1)S(1)} %get-tuple-element.63), channel_id=1, source_target_pairs={{0,4},{1,5},{2,6},{3,7},{4,0},{5,1},{6,2},{7,3},{8,12},{9,13},{10,... | collective-permute-start | bytes 1966088 | tf_op jit(solution)/shard_map/ppermute | solution.py:27
  74.9 6.1 %collective-permute-start.28 = (bf16[8,40,1024]{2,1,0:T(8,128)(2,1)S(1)}, bf16[8,40,1024]{2,1,0:T(8,128)(2,1)S(1)}, u32[]{:S(2)}, u32[]{:S(2)}) collective-permute-start(bf16[8,40,1024]{2,1,0:T(8,128)(2,1)S(1)} %get-tuple-element.64), channel_id=1, source_target_pairs={{0,1},{1,0},{2,3},{3,2},{4,5},{5,4},{6,7},{7,6},{8,9},{9,8},{10,11... | collective-permute-start | bytes 1966088 | tf_op jit(solution)/shard_map/ppermute | solution.py:27
  76.0 17.6 %collective-permute-start.30 = (bf16[8,40,1024]{2,1,0:T(8,128)(2,1)S(1)}, bf16[8,40,1024]{2,1,0:T(8,128)(2,1)}, u32[]{:S(2)}, u32[]{:S(2)}) collective-permute-start(bf16[8,40,1024]{2,1,0:T(8,128)(2,1)S(1)} %get-tuple-element.64), channel_id=1, source_target_pairs={{0,2},{1,3},{2,0},{3,1},{4,6},{5,7},{6,4},{7,5},{8,10},{9,11},{10,... | collective-permute-start | bytes 1966088 | tf_op jit(solution)/shard_map/ppermute | solution.py:27
  81.1 16.8 %collective-permute-start.8 = (bf16[8,40,1024]{2,1,0:T(8,128)(2,1)}, bf16[8,40,1024]{2,1,0:T(8,128)(2,1)S(1)}, u32[]{:S(2)}, u32[]{:S(2)}) collective-permute-start(bf16[8,40,1024]{2,1,0:T(8,128)(2,1)} %collective-permute-done.6), channel_id=1, source_target_pairs={{0,1},{1,0},{2,3},{3,2},{4,5},{5,4},{6,7},{7,6},{8,9},{9,8},{10,11... | collective-permute-start | bytes 1966088 | tf_op jit(solution)/shard_map/ppermute | solution.py:27
  82.4 21.7 %collective-permute-start.10 = (bf16[8,40,1024]{2,1,0:T(8,128)(2,1)}, bf16[8,40,1024]{2,1,0:T(8,128)(2,1)S(1)}, u32[]{:S(2)}, u32[]{:S(2)}) collective-permute-start(bf16[8,40,1024]{2,1,0:T(8,128)(2,1)} %collective-permute-done.2), channel_id=1, source_target_pairs={{0,4},{1,5},{2,6},{3,7},{4,0},{5,1},{6,2},{7,3},{8,12},{9,13},{10,... | collective-permute-start | bytes 1966088 | tf_op jit(solution)/shard_map/ppermute | solution.py:27
  84.6 22.6 %collective-permute-start.11 = (bf16[8,40,1024]{2,1,0:T(8,128)(2,1)}, bf16[8,40,1024]{2,1,0:T(8,128)(2,1)S(1)}, u32[]{:S(2)}, u32[]{:S(2)}) collective-permute-start(bf16[8,40,1024]{2,1,0:T(8,128)(2,1)} %collective-permute-done.7), channel_id=1, source_target_pairs={{0,2},{1,3},{2,0},{3,1},{4,6},{5,7},{6,4},{7,5},{8,10},{9,11},{10,... | collective-permute-start | bytes 1966088 | tf_op jit(solution)/shard_map/ppermute | solution.py:27
  93.6 13.6 %collective-permute-start.9 = (bf16[8,40,1024]{2,1,0:T(8,128)(2,1)}, bf16[8,40,1024]{2,1,0:T(8,128)(2,1)S(1)}, u32[]{:S(2)}, u32[]{:S(2)}) collective-permute-start(bf16[8,40,1024]{2,1,0:T(8,128)(2,1)} %collective-permute-done.7), channel_id=1, source_target_pairs={{0,1},{1,0},{2,3},{3,2},{4,5},{5,4},{6,7},{7,6},{8,9},{9,8},{10,11... | collective-permute-start | bytes 1966088 | tf_op jit(solution)/shard_map/ppermute | solution.py:27
  97.9 37.2 %collective-permute-start.34 = (bf16[8,40,1024]{2,1,0:T(8,128)(2,1)S(1)}, bf16[8,40,1024]{2,1,0:T(8,128)(2,1)}, u32[]{:S(2)}, u32[]{:S(2)}) collective-permute-start(bf16[8,40,1024]{2,1,0:T(8,128)(2,1)S(1)} %get-tuple-element.64), channel_id=1, source_target_pairs={{0,4},{1,5},{2,6},{3,7},{4,0},{5,1},{6,2},{7,3},{8,12},{9,13},{10,... | collective-permute-start | bytes 1966088 | tf_op jit(solution)/shard_map/ppermute | solution.py:27
  104.1 33.4 %collective-permute-start.33 = (bf16[8,40,1024]{2,1,0:T(8,128)(2,1)}, bf16[8,40,1024]{2,1,0:T(8,128)(2,1)}, u32[]{:S(2)}, u32[]{:S(2)}) collective-permute-start(bf16[8,40,1024]{2,1,0:T(8,128)(2,1)} %collective-permute-done.31), channel_id=1, source_target_pairs={{0,1},{1,0},{2,3},{3,2},{4,5},{5,4},{6,7},{7,6},{8,9},{9,8},{10,11... | collective-permute-start | bytes 1966088 | tf_op jit(solution)/shard_map/ppermute | solution.py:27
  107.2 4.5 %collective-permute-start.12 = (bf16[8,40,1024]{2,1,0:T(8,128)(2,1)S(1)}, bf16[8,40,1024]{2,1,0:T(8,128)(2,1)S(1)}, u32[]{:S(2)}, u32[]{:S(2)}) collective-permute-start(bf16[8,40,1024]{2,1,0:T(8,128)(2,1)S(1)} %collective-permute-done.10), channel_id=1, source_target_pairs={{0,1},{1,0},{2,3},{3,2},{4,5},{5,4},{6,7},{7,6},{8,9},{9,8},{10,11... | collective-permute-start | bytes 1966088 | tf_op jit(solution)/shard_map/ppermute | solution.py:27
  107.2 5.6 %collective-permute-start.13 = (bf16[8,40,1024]{2,1,0:T(8,128)(2,1)S(1)}, bf16[8,40,1024]{2,1,0:T(8,128)(2,1)S(1)}, u32[]{:S(2)}, u32[]{:S(2)}) collective-permute-start(bf16[8,40,1024]{2,1,0:T(8,128)(2,1)S(1)} %collective-permute-done.11), channel_id=1, source_target_pairs={{0,1},{1,0},{2,3},{3,2},{4,5},{5,4},{6,7},{7,6},{8,9},{9,8},{10,11... | collective-permute-start | bytes 1966088 | tf_op jit(solution)/shard_map/ppermute | solution.py:27
  107.7 41.0 %collective-permute-start.39 = (bf16[8,40,1024]{2,1,0:T(8,128)(2,1)}, bf16[8,40,1024]{2,1,0:T(8,128)(2,1)}, u32[]{:S(2)}, u32[]{:S(2)}) collective-permute-start(bf16[8,40,1024]{2,1,0:T(8,128)(2,1)} %collective-permute-done.35), channel_id=1, source_target_pairs={{0,2},{1,3},{2,0},{3,1},{4,6},{5,7},{6,4},{7,5},{8,10},{9,11},{10,... | collective-permute-start | bytes 1966088 | tf_op jit(solution)/shard_map/ppermute | solution.py:27
  111.6 37.6 %collective-permute-start.37 = (bf16[8,40,1024]{2,1,0:T(8,128)(2,1)}, bf16[8,40,1024]{2,1,0:T(8,128)(2,1)}, u32[]{:S(2)}, u32[]{:S(2)}) collective-permute-start(bf16[8,40,1024]{2,1,0:T(8,128)(2,1)} %collective-permute-done.35), channel_id=1, source_target_pairs={{0,1},{1,0},{2,3},{3,2},{4,5},{5,4},{6,7},{7,6},{8,9},{9,8},{10,11... | collective-permute-start | bytes 1966088 | tf_op jit(solution)/shard_map/ppermute | solution.py:27
  112.8 23.6 %collective-permute-start.32 = (bf16[8,40,1024]{2,1,0:T(8,128)(2,1)}, bf16[8,40,1024]{2,1,0:T(8,128)(2,1)S(1)}, u32[]{:S(2)}, u32[]{:S(2)}) collective-permute-start(bf16[8,40,1024]{2,1,0:T(8,128)(2,1)} %collective-permute-done.30), channel_id=1, source_target_pairs={{0,1},{1,0},{2,3},{3,2},{4,5},{5,4},{6,7},{7,6},{8,9},{9,8},{10,11... | collective-permute-start | bytes 1966088 | tf_op jit(solution)/shard_map/ppermute | solution.py:27
  123.8 34.4 %copy-start.34 = (bf16[8,20,1024]{2,0,1:T(8,128)(2,1)}, bf16[8,20,1024]{2,0,1:T(8,128)(2,1)S(1)}, u32[]{:S(2)}) copy-start(bf16[8,20,1024]{2,0,1:T(8,128)(2,1)S(1)} %get-tuple-element.59) | copy-start | bytes 983044
  123.8 40.9 %copy-start.40 = (bf16[8,20,1024]{2,0,1:T(8,128)(2,1)}, bf16[8,20,1024]{2,0,1:T(8,128)(2,1)S(1)}, u32[]{:S(2)}) copy-start(bf16[8,20,1024]{2,0,1:T(8,128)(2,1)S(1)} %get-tuple-element.51) | copy-start | bytes 983044
  123.8 44.4 %copy-start.32 = (bf16[8,20,1024]{2,0,1:T(8,128)(2,1)}, bf16[8,20,1024]{2,0,1:T(8,128)(2,1)S(1)}, u32[]{:S(2)}) copy-start(bf16[8,20,1024]{2,0,1:T(8,128)(2,1)S(1)} %get-tuple-element.55) | copy-start | bytes 983044
  123.8 44.8 %copy-start.36 = (bf16[8,20,1024]{2,0,1:T(8,128)(2,1)}, bf16[8,20,1024]{2,0,1:T(8,128)(2,1)S(1)}, u32[]{:S(2)}) copy-start(bf16[8,20,1024]{2,0,1:T(8,128)(2,1)S(1)} %get-tuple-element.47) | copy-start | bytes 983044
  135.1 16.9 %collective-permute-start.38 = (bf16[8,40,1024]{2,1,0:T(8,128)(2,1)}, bf16[8,40,1024]{2,1,0:T(8,128)(2,1)S(1)}, u32[]{:S(2)}, u32[]{:S(2)}) collective-permute-start(bf16[8,40,1024]{2,1,0:T(8,128)(2,1)} %collective-permute-done.30), channel_id=1, source_target_pairs={{0,4},{1,5},{2,6},{3,7},{4,0},{5,1},{6,2},{7,3},{8,12},{9,13},{10,... | collective-permute-start | bytes 1966088 | tf_op jit(solution)/shard_map/ppermute | solution.py:27
  136.4 9.3 %collective-permute-start.36 = (bf16[8,40,1024]{2,1,0:T(8,128)(2,1)}, bf16[8,40,1024]{2,1,0:T(8,128)(2,1)S(1)}, u32[]{:S(2)}, u32[]{:S(2)}) collective-permute-start(bf16[8,40,1024]{2,1,0:T(8,128)(2,1)} %collective-permute-done.34), channel_id=1, source_target_pairs={{0,1},{1,0},{2,3},{3,2},{4,5},{5,4},{6,7},{7,6},{8,9},{9,8},{10,11... | collective-permute-start | bytes 1966088 | tf_op jit(solution)/shard_map/ppermute | solution.py:27
  137.4 138.2 %collective-permute-start.17 = (bf16[8,40,1024]{2,1,0:T(8,128)(2,1)}, bf16[8,40,1024]{2,1,0:T(8,128)(2,1)}, u32[]{:S(2)}, u32[]{:S(2)}) collective-permute-start(bf16[8,40,1024]{2,1,0:T(8,128)(2,1)} %convolution_convert_fusion.27), channel_id=1, source_target_pairs={{0,1},{1,0},{2,3},{3,2},{4,5},{5,4},{6,7},{7,6},{8,9},{9,8},{10,11... | collective-permute-start | bytes 1966088 | tf_op jit(solution)/shard_map/ppermute | solution.py:27
  145.7 94.6 %collective-permute-start.22 = (bf16[8,40,1024]{2,1,0:T(8,128)(2,1)}, bf16[8,40,1024]{2,1,0:T(8,128)(2,1)}, u32[]{:S(2)}, u32[]{:S(2)}) collective-permute-start(bf16[8,40,1024]{2,1,0:T(8,128)(2,1)} %convolution_convert_fusion.21), channel_id=1, source_target_pairs={{0,1},{1,0},{2,3},{3,2},{4,5},{5,4},{6,7},{7,6},{8,9},{9,8},{10,11... | collective-permute-start | bytes 1966088 | tf_op jit(solution)/shard_map/ppermute | solution.py:27
  148.7 105.9 %collective-permute-start.15 = (bf16[8,40,1024]{2,1,0:T(8,128)(2,1)}, bf16[8,40,1024]{2,1,0:T(8,128)(2,1)}, u32[]{:S(2)}, u32[]{:S(2)}) collective-permute-start(bf16[8,40,1024]{2,1,0:T(8,128)(2,1)} %convolution_convert_fusion.29), channel_id=1, source_target_pairs={{0,1},{1,0},{2,3},{3,2},{4,5},{5,4},{6,7},{7,6},{8,9},{9,8},{10,11... | collective-permute-start | bytes 1966088 | tf_op jit(solution)/shard_map/ppermute | solution.py:27
  149.2 23.9 %collective-permute-start.41 = (bf16[8,40,1024]{2,1,0:T(8,128)(2,1)}, bf16[8,40,1024]{2,1,0:T(8,128)(2,1)S(1)}, u32[]{:S(2)}, u32[]{:S(2)}) collective-permute-start(bf16[8,40,1024]{2,1,0:T(8,128)(2,1)} %collective-permute-done.39), channel_id=1, source_target_pairs={{0,1},{1,0},{2,3},{3,2},{4,5},{5,4},{6,7},{7,6},{8,9},{9,8},{10,11... | collective-permute-start | bytes 1966088 | tf_op jit(solution)/shard_map/ppermute | solution.py:27
  152.1 19.5 %collective-permute-start.40 = (bf16[8,40,1024]{2,1,0:T(8,128)(2,1)S(1)}, bf16[8,40,1024]{2,1,0:T(8,128)(2,1)S(1)}, u32[]{:S(2)}, u32[]{:S(2)}) collective-permute-start(bf16[8,40,1024]{2,1,0:T(8,128)(2,1)S(1)} %collective-permute-done.38), channel_id=1, source_target_pairs={{0,1},{1,0},{2,3},{3,2},{4,5},{5,4},{6,7},{7,6},{8,9},{9,8},{10,11... | collective-permute-start | bytes 1966088 | tf_op jit(solution)/shard_map/ppermute | solution.py:27
  171.6 108.4 %collective-permute-start.24 = (bf16[8,40,1024]{2,1,0:T(8,128)(2,1)}, bf16[8,40,1024]{2,1,0:T(8,128)(2,1)}, u32[]{:S(2)}, u32[]{:S(2)}) collective-permute-start(bf16[8,40,1024]{2,1,0:T(8,128)(2,1)} %convolution_convert_fusion.19), channel_id=1, source_target_pairs={{0,1},{1,0},{2,3},{3,2},{4,5},{5,4},{6,7},{7,6},{8,9},{9,8},{10,11... | collective-permute-start | bytes 1966088 | tf_op jit(solution)/shard_map/ppermute | solution.py:27
  173.1 69.7 %collective-permute-start.25 = (bf16[8,40,1024]{2,1,0:T(8,128)(2,1)}, bf16[8,40,1024]{2,1,0:T(8,128)(2,1)}, u32[]{:S(2)}, u32[]{:S(2)}) collective-permute-start(bf16[8,40,1024]{2,1,0:T(8,128)(2,1)} %convolution_convert_fusion.17), channel_id=1, source_target_pairs={{0,1},{1,0},{2,3},{3,2},{4,5},{5,4},{6,7},{7,6},{8,9},{9,8},{10,11... | collective-permute-start | bytes 1966088 | tf_op jit(solution)/shard_map/ppermute | solution.py:27
  184.9 30.2 %copy-start.44 = (bf16[8,20,1024]{2,0,1:T(8,128)(2,1)}, bf16[8,20,1024]{2,0,1:T(8,128)(2,1)S(1)}, u32[]{:S(2)}) copy-start(bf16[8,20,1024]{2,0,1:T(8,128)(2,1)S(1)} %get-tuple-element.31) | copy-start | bytes 983044
  233.3 44.0 %all-to-all-start.1 = ((bf16[8,32,800]{2,1,0:T(8,128)(2,1)}), bf16[8,32,800]{2,1,0:T(8,128)(2,1)S(1)}, u32[]{:S(2)}, u32[]{:S(2)}) async-start(bf16[8,32,800]{2,1,0:T(8,128)(2,1)} %constant_dynamic-update-slice_fusion.2), calls=%async_computation.1 | async-start | bytes 917504 | tf_op jit(solution)/shard_map/all_to_all | solution.py:141
  237.8 155.8 %all-reduce.3.cloned.1.call-start = ((), (), s32[]{:S(2)}) async-start(), calls=%async_computation.2 | async-start | bytes 5767168 | tf_op jit(solution)/shard_map/psum | solution.py:142
  240.3 27.2 %collective-permute-start.18 = (bf16[8,40,1024]{2,1,0:T(8,128)(2,1)}, bf16[8,40,1024]{2,1,0:T(8,128)(2,1)}, u32[]{:S(2)}, u32[]{:S(2)}) collective-permute-start(bf16[8,40,1024]{2,1,0:T(8,128)(2,1)} %convolution_convert_fusion.25), channel_id=1, source_target_pairs={{0,1},{1,0},{2,3},{3,2},{4,5},{5,4},{6,7},{7,6},{8,9},{9,8},{10,11... | collective-permute-start | bytes 1966088 | tf_op jit(solution)/shard_map/ppermute | solution.py:27
  242.8 42.2 %collective-permute-start.21 = (bf16[8,40,1024]{2,1,0:T(8,128)(2,1)}, bf16[8,40,1024]{2,1,0:T(8,128)(2,1)}, u32[]{:S(2)}, u32[]{:S(2)}) collective-permute-start(bf16[8,40,1024]{2,1,0:T(8,128)(2,1)} %convolution_convert_fusion.23), channel_id=1, source_target_pairs={{0,1},{1,0},{2,3},{3,2},{4,5},{5,4},{6,7},{7,6},{8,9},{9,8},{10,11... | collective-permute-start | bytes 1966088 | tf_op jit(solution)/shard_map/ppermute | solution.py:27
  254.7 25.5 %collective-permute-start.26 = (bf16[8,40,1024]{2,1,0:T(8,128)(2,1)}, bf16[8,40,1024]{2,1,0:T(8,128)(2,1)}, u32[]{:S(2)}, u32[]{:S(2)}) collective-permute-start(bf16[8,40,1024]{2,1,0:T(8,128)(2,1)} %add_convert_fusion.16), channel_id=1, source_target_pairs={{0,4},{1,5},{2,6},{3,7},{4,0},{5,1},{6,2},{7,3},{8,12},{9,13},{10,... | collective-permute-start | bytes 1966088 | tf_op jit(solution)/shard_map/ppermute | solution.py:27
  267.5 13.2 %collective-permute-start.43 = (bf16[8,40,1024]{2,1,0:T(8,128)(2,1)}, bf16[8,40,1024]{2,1,0:T(8,128)(2,1)}, u32[]{:S(2)}, u32[]{:S(2)}) collective-permute-start(bf16[8,40,1024]{2,1,0:T(8,128)(2,1)} %convolution_convert_fusion.13), channel_id=1, source_target_pairs={{0,1},{1,0},{2,3},{3,2},{4,5},{5,4},{6,7},{7,6},{8,9},{9,8},{10,11... | collective-permute-start | bytes 1966088 | tf_op jit(solution)/shard_map/ppermute | solution.py:27
  275.6 10.1 %collective-permute-start.53 = (bf16[8,40,1024]{2,1,0:T(8,128)(2,1)}, bf16[8,40,1024]{2,1,0:T(8,128)(2,1)}, u32[]{:S(2)}, u32[]{:S(2)}) collective-permute-start(bf16[8,40,1024]{2,1,0:T(8,128)(2,1)} %convolution_convert_fusion.1), channel_id=1, source_target_pairs={{0,1},{1,0},{2,3},{3,2},{4,5},{5,4},{6,7},{7,6},{8,9},{9,8},{10,11... | collective-permute-start | bytes 1966088 | tf_op jit(solution)/shard_map/ppermute | solution.py:27
  280.0 7.5 %collective-permute-start.14 = (bf16[8,40,1024]{2,1,0:T(8,128)(2,1)}, bf16[8,40,1024]{2,1,0:T(8,128)(2,1)S(1)}, u32[]{:S(2)}, u32[]{:S(2)}) collective-permute-start(bf16[8,40,1024]{2,1,0:T(8,128)(2,1)} %convolution_convert_fusion.31), channel_id=1, source_target_pairs={{0,1},{1,0},{2,3},{3,2},{4,5},{5,4},{6,7},{7,6},{8,9},{9,8},{10,11... | collective-permute-start | bytes 1966088 | tf_op jit(solution)/shard_map/ppermute | solution.py:27
  280.2 17.3 %collective-permute-start.19 = (bf16[8,40,1024]{2,1,0:T(8,128)(2,1)}, bf16[8,40,1024]{2,1,0:T(8,128)(2,1)S(1)}, u32[]{:S(2)}, u32[]{:S(2)}) collective-permute-start(bf16[8,40,1024]{2,1,0:T(8,128)(2,1)} %add_convert_fusion.23), channel_id=1, source_target_pairs={{0,2},{1,3},{2,0},{3,1},{4,6},{5,7},{6,4},{7,5},{8,10},{9,11},{10,... | collective-permute-start | bytes 1966088 | tf_op jit(solution)/shard_map/ppermute | solution.py:27
  280.7 17.3 %collective-permute-start.46 = (bf16[8,40,1024]{2,1,0:T(8,128)(2,1)}, bf16[8,40,1024]{2,1,0:T(8,128)(2,1)S(1)}, u32[]{:S(2)}, u32[]{:S(2)}) collective-permute-start(bf16[8,40,1024]{2,1,0:T(8,128)(2,1)} %convolution_convert_fusion.9), channel_id=1, source_target_pairs={{0,1},{1,0},{2,3},{3,2},{4,5},{5,4},{6,7},{7,6},{8,9},{9,8},{10,11... | collective-permute-start | bytes 1966088 | tf_op jit(solution)/shard_map/ppermute | solution.py:27
  285.1 17.6 %collective-permute-start.23 = (bf16[8,40,1024]{2,1,0:T(8,128)(2,1)S(1)}, bf16[8,40,1024]{2,1,0:T(8,128)(2,1)S(1)}, u32[]{:S(2)}, u32[]{:S(2)}) collective-permute-start(bf16[8,40,1024]{2,1,0:T(8,128)(2,1)S(1)} %copy-done.56), channel_id=1, source_target_pairs={{0,4},{1,5},{2,6},{3,7},{4,0},{5,1},{6,2},{7,3},{8,12},{9,13},{10,... | collective-permute-start | bytes 1966088 | tf_op jit(solution)/shard_map/ppermute | solution.py:27
  285.7 17.0 %collective-permute-start.50 = (bf16[8,40,1024]{2,1,0:T(8,128)(2,1)S(1)}, bf16[8,40,1024]{2,1,0:T(8,128)(2,1)S(1)}, u32[]{:S(2)}, u32[]{:S(2)}) collective-permute-start(bf16[8,40,1024]{2,1,0:T(8,128)(2,1)S(1)} %copy-done.75), channel_id=1, source_target_pairs={{0,1},{1,0},{2,3},{3,2},{4,5},{5,4},{6,7},{7,6},{8,9},{9,8},{10,11... | collective-permute-start | bytes 1966088 | tf_op jit(solution)/shard_map/ppermute | solution.py:27
  287.5 18.1 %collective-permute-start.52 = (bf16[8,40,1024]{2,1,0:T(8,128)(2,1)S(1)}, bf16[8,40,1024]{2,1,0:T(8,128)(2,1)S(1)}, u32[]{:S(2)}, u32[]{:S(2)}) collective-permute-start(bf16[8,40,1024]{2,1,0:T(8,128)(2,1)S(1)} %copy-done.85), channel_id=1, source_target_pairs={{0,1},{1,0},{2,3},{3,2},{4,5},{5,4},{6,7},{7,6},{8,9},{9,8},{10,11... | collective-permute-start | bytes 1966088 | tf_op jit(solution)/shard_map/ppermute | solution.py:27
  297.4 18.7 %collective-permute-start.54 = (bf16[8,40,1024]{2,1,0:T(8,128)(2,1)S(1)}, bf16[8,40,1024]{2,1,0:T(8,128)(2,1)S(1)}, u32[]{:S(2)}, u32[]{:S(2)}) collective-permute-start(bf16[8,40,1024]{2,1,0:T(8,128)(2,1)S(1)} %add_convert_fusion.2), channel_id=1, source_target_pairs={{0,4},{1,5},{2,6},{3,7},{4,0},{5,1},{6,2},{7,3},{8,12},{9,13},{10,... | collective-permute-start | bytes 1966088 | tf_op jit(solution)/shard_map/ppermute | solution.py:27
  298.0 18.2 %collective-permute-start.27 = (bf16[8,40,1024]{2,1,0:T(8,128)(2,1)S(1)}, bf16[8,40,1024]{2,1,0:T(8,128)(2,1)S(1)}, u32[]{:S(2)}, u32[]{:S(2)}) collective-permute-start(bf16[8,40,1024]{2,1,0:T(8,128)(2,1)S(1)} %add_convert_fusion.15), channel_id=1, source_target_pairs={{0,2},{1,3},{2,0},{3,1},{4,6},{5,7},{6,4},{7,5},{8,10},{9,11},{10,... | collective-permute-start | bytes 1966088 | tf_op jit(solution)/shard_map/ppermute | solution.py:27
  302.7 17.1 %collective-permute-start.45 = (bf16[8,40,1024]{2,1,0:T(8,128)(2,1)S(1)}, bf16[8,40,1024]{2,1,0:T(8,128)(2,1)S(1)}, u32[]{:S(2)}, u32[]{:S(2)}) collective-permute-start(bf16[8,40,1024]{2,1,0:T(8,128)(2,1)S(1)} %copy-done.83), channel_id=1, source_target_pairs={{0,1},{1,0},{2,3},{3,2},{4,5},{5,4},{6,7},{7,6},{8,9},{9,8},{10,11... | collective-permute-start | bytes 1966088 | tf_op jit(solution)/shard_map/ppermute | solution.py:27
  302.7 27.0 %collective-permute-start.47 = (bf16[8,40,1024]{2,1,0:T(8,128)(2,1)S(1)}, bf16[8,40,1024]{2,1,0:T(8,128)(2,1)S(1)}, u32[]{:S(2)}, u32[]{:S(2)}) collective-permute-start(bf16[8,40,1024]{2,1,0:T(8,128)(2,1)S(1)} %add_convert_fusion.9), channel_id=1, source_target_pairs={{0,2},{1,3},{2,0},{3,1},{4,6},{5,7},{6,4},{7,5},{8,10},{9,11},{10,... | collective-permute-start | bytes 1966088 | tf_op jit(solution)/shard_map/ppermute | solution.py:27
  305.6 38.2 %collective-permute-start.16 = (bf16[8,40,1024]{2,1,0:T(8,128)(2,1)S(1)}, bf16[8,40,1024]{2,1,0:T(8,128)(2,1)S(1)}, u32[]{:S(2)}, u32[]{:S(2)}) collective-permute-start(bf16[8,40,1024]{2,1,0:T(8,128)(2,1)S(1)} %copy-done.55), channel_id=1, source_target_pairs={{0,2},{1,3},{2,0},{3,1},{4,6},{5,7},{6,4},{7,5},{8,10},{9,11},{10,... | collective-permute-start | bytes 1966088 | tf_op jit(solution)/shard_map/ppermute | solution.py:27
  316.2 27.6 %collective-permute-start.49 = (bf16[8,40,1024]{2,1,0:T(8,128)(2,1)S(1)}, bf16[8,40,1024]{2,1,0:T(8,128)(2,1)S(1)}, u32[]{:S(2)}, u32[]{:S(2)}) collective-permute-start(bf16[8,40,1024]{2,1,0:T(8,128)(2,1)S(1)} %copy-done.80), channel_id=1, source_target_pairs={{0,1},{1,0},{2,3},{3,2},{4,5},{5,4},{6,7},{7,6},{8,9},{9,8},{10,11... | collective-permute-start | bytes 1966088 | tf_op jit(solution)/shard_map/ppermute | solution.py:27
  316.2 28.0 %collective-permute-start.20 = (bf16[8,40,1024]{2,1,0:T(8,128)(2,1)S(1)}, bf16[8,40,1024]{2,1,0:T(8,128)(2,1)S(1)}, u32[]{:S(2)}, u32[]{:S(2)}) collective-permute-start(bf16[8,40,1024]{2,1,0:T(8,128)(2,1)S(1)} %add_convert_fusion.22), channel_id=1, source_target_pairs={{0,4},{1,5},{2,6},{3,7},{4,0},{5,1},{6,2},{7,3},{8,12},{9,13},{10,... | collective-permute-start | bytes 1966088 | tf_op jit(solution)/shard_map/ppermute | solution.py:27
  319.8 28.0 %collective-permute-start.51 = (bf16[8,40,1024]{2,1,0:T(8,128)(2,1)}, bf16[8,40,1024]{2,1,0:T(8,128)(2,1)}, u32[]{:S(2)}, u32[]{:S(2)}) collective-permute-start(bf16[8,40,1024]{2,1,0:T(8,128)(2,1)} %add_convert_fusion.5), channel_id=1, source_target_pairs={{0,4},{1,5},{2,6},{3,7},{4,0},{5,1},{6,2},{7,3},{8,12},{9,13},{10,... | collective-permute-start | bytes 1966088 | tf_op jit(solution)/shard_map/ppermute | solution.py:27
  329.7 28.2 %collective-permute-start.55 = (bf16[8,40,1024]{2,1,0:T(8,128)(2,1)}, bf16[8,40,1024]{2,1,0:T(8,128)(2,1)}, u32[]{:S(2)}, u32[]{:S(2)}) collective-permute-start(bf16[8,40,1024]{2,1,0:T(8,128)(2,1)} %add_convert_fusion.1), channel_id=1, source_target_pairs={{0,2},{1,3},{2,0},{3,1},{4,6},{5,7},{6,4},{7,5},{8,10},{9,11},{10,... | collective-permute-start | bytes 1966088 | tf_op jit(solution)/shard_map/ppermute | solution.py:27
  343.7 16.1 %collective-permute-start.42 = (bf16[8,40,1024]{2,1,0:T(8,128)(2,1)}, bf16[8,40,1024]{2,1,0:T(8,128)(2,1)}, u32[]{:S(2)}, u32[]{:S(2)}) collective-permute-start(bf16[8,40,1024]{2,1,0:T(8,128)(2,1)} %convolution_convert_fusion.15), channel_id=1, source_target_pairs={{0,1},{1,0},{2,3},{3,2},{4,5},{5,4},{6,7},{7,6},{8,9},{9,8},{10,11... | collective-permute-start | bytes 1966088 | tf_op jit(solution)/shard_map/ppermute | solution.py:27
  343.7 26.6 %collective-permute-start.44 = (bf16[8,40,1024]{2,1,0:T(8,128)(2,1)}, bf16[8,40,1024]{2,1,0:T(8,128)(2,1)}, u32[]{:S(2)}, u32[]{:S(2)}) collective-permute-start(bf16[8,40,1024]{2,1,0:T(8,128)(2,1)} %add_convert_fusion.12), channel_id=1, source_target_pairs={{0,2},{1,3},{2,0},{3,1},{4,6},{5,7},{6,4},{7,5},{8,10},{9,11},{10,... | collective-permute-start | bytes 1966088 | tf_op jit(solution)/shard_map/ppermute | solution.py:27
  344.1 26.2 %collective-permute-start.48 = (bf16[8,40,1024]{2,1,0:T(8,128)(2,1)}, bf16[8,40,1024]{2,1,0:T(8,128)(2,1)}, u32[]{:S(2)}, u32[]{:S(2)}) collective-permute-start(bf16[8,40,1024]{2,1,0:T(8,128)(2,1)} %add_convert_fusion.8), channel_id=1, source_target_pairs={{0,4},{1,5},{2,6},{3,7},{4,0},{5,1},{6,2},{7,3},{8,12},{9,13},{10,... | collective-permute-start | bytes 1966088 | tf_op jit(solution)/shard_map/ppermute | solution.py:27
  (85 other events, 680.7 us)
Sparse Core Ops, SparseCore 0:
  280.1 113.5 all-reduce.2
